TPU v7x, 32 devices: a whole 2x2x4 slice. The times are simulated.
32 devices in a mesh: gx: 4 (over y, core), gy: 8 (over z, x).
Axes of the slice: x: 2, y: 2, z: 4, core: 2. Of those that a mesh axis runs over, the one named last changes fastest.
Arguments:
- conserved: float32 [5, 1, 1536, 1024], P(None, None, 'gx', 'gy'), may hold values from -0.375 to 3.33, as said below
- time_step: float32 [1, 1536, 1024], P(None, 'gx', 'gy'), may hold values from 200 to 1600
Outputs:
- update: float32 [5, 1, 1536, 1024], P(None, None, 'gx', 'gy')
Inputs may be any that keep to these rules, and one draw needn't show every extreme that they name: conserved holds the conserved variables of a gas with heat ratio 1.4; density and pressure lie within 0.8 to 1.25 and each velocity component within -0.3 to 0.3.
All inputs are finite; a program needn't handle non-finite values.
Results may differ from a plain program's by a relative error of at most 0.0003.
Values sent between devices are 32-bit elements; how exact they have to be, the bound alone decides.
A program may use at most 128 MiB of HBM per device.

v0:
```python
import functools
import jax
import jax.numpy as jnp
from jax import lax
from jax.experimental import pallas as pl
from jax.experimental.pallas import tpu as pltpu
from jax.sharding import PartitionSpec as P

EPS = 0.02
MESH = pl.DeviceIdType.MESH
ROWS_PACK = 72
FAMILY = (0, 0, 0, 1, 2)


def primitive(q):
    inv = 1.0 / q[0]
    u = q[1] * inv
    v = q[2] * inv
    w = q[3] * inv
    p = 0.4 * (q[4] - 0.5 * (q[1] * u + q[2] * v + q[3] * w))
    c2 = 1.4 * p * inv
    return u, v, w, p, c2


def flux_x(q, u, p):
    return [q[1], q[1] * u + p, q[2] * u, q[3] * u, (q[4] + p) * u]


def flux_y(q, v, p):
    return [q[2], q[1] * v, q[2] * v + p, q[3] * v, (q[4] + p) * v]


def mm(a, b):
    return (
        a[0] * b[0] + a[1] * b[2],
        a[0] * b[1] + a[1] * b[3],
        a[2] * b[0] + a[3] * b[2],
        a[2] * b[1] + a[3] * b[3],
    )


def mv(a, x):
    return (a[0] * x[0] + a[1] * x[1], a[2] * x[0] + a[3] * x[1])


def add(a, b):
    return tuple(x + y for x, y in zip(a, b))


def schur_inverse(x, y):
    pr = mm(y, x)
    m0, m1, m2, m3 = 1.0 - pr[0], -pr[1], -pr[2], 1.0 - pr[3]
    r = 1.0 / (m0 * m3 - m1 * m2)
    return (m3 * r, -m1 * r, -m2 * r, m0 * r)


def merge(mats_a, mats_b, rhs_a, rhs_b, last=False):
    mats, rec_m, invs = [], [], []
    for (hl_a, hr_a, tl_a, tr_a), (hl_b, hr_b, tl_b, tr_b) in zip(mats_a, mats_b):
        minv = schur_inverse(tr_a, hl_b)
        invs.append(minv)
        if last:
            continue
        head_l = mm(minv, mm(hl_b, tl_a))
        head_r = mm(minv, hr_b)
        tail_l = add(tl_a, mm(tr_a, head_l))
        tail_r = mm(tr_a, head_r)
        mats.append(
            (
                add(hl_a, mm(hr_a, head_l)),
                mm(hr_a, head_r),
                mm(tl_b, tail_l),
                add(tr_b, mm(tl_b, tail_r)),
            )
        )
        rec_m.append((head_l, head_r, tail_l, tail_r))
    rhs, rec_y = [], []
    for f, ((h_a, t_a), (h_b, t_b)) in enumerate(zip(rhs_a, rhs_b)):
        m = FAMILY[f]
        hl_b, tr_a = mats_b[m][0], mats_a[m][3]
        head_y = mv(invs[m], add(h_b, mv(hl_b, t_a)))
        tail_y = add(t_a, mv(tr_a, head_y))
        rec_y.append((head_y, tail_y))
        if not last:
            rhs.append((add(h_a, mv(mats_a[m][1], head_y)), add(t_b, mv(mats_b[m][2], tail_y))))
    return mats, rhs, (rec_m, rec_y)


def shifted(tree, d):
    return jax.tree.map(lambda x: pltpu.roll(x, 8 - d, 0), tree)


def reduce_levels(mats, rhs, strides, root):
    records = []
    for d in strides:
        last = root and d == strides[-1]
        mats, rhs, rec = merge(mats, shifted(mats, d), rhs, shifted(rhs, d), last)
        records.append(rec)
    return mats, rhs, records


def expand_levels(records, strides, left, right, sub, root):
    for d, (rec_m, rec_y) in reversed(list(zip(strides, records))):
        upper = (sub & d) != 0
        for f in range(5):
            head, tail = rec_y[f]
            if left[f] is not None:
                hl, hr, tl, tr = rec_m[FAMILY[f]]
                head = add(add(head, mv(hl, left[f])), mv(hr, right[f]))
                tail = add(add(tail, mv(tl, left[f])), mv(tr, right[f]))
                lo, hi = left[f], right[f]
            else:
                lo = hi = (jnp.zeros_like(head[0]),) * 2
            left[f] = tuple(jnp.where(upper, pltpu.roll(x, d, 0), y) for x, y in zip(tail, lo))
            right[f] = tuple(jnp.where(upper, pltpu.roll(y, d, 0), x) for x, y in zip(head, hi))
    return left, right


def kernel(
    nx, ny, rows,
    q_hbm, dt_hbm, out_hbm,
    qin, dtin, oout, hl, hr, eqs, fs, us, vs, ws, cs, rcs, res, mat, gs,
    wsend, wl, wr, pack, gath,
    in_sem, out_sem, hx_send, hx_recv, wy_send, wy_recv, g_send, g_recv,
):
    T = rows // 8
    ix = lax.axis_index("gx")
    iy = lax.axis_index("gy")
    has_l, has_r = ix > 0, ix < nx - 1
    has_d, has_u = iy > 0, iy < ny - 1
    cp_q = pltpu.make_async_copy(q_hbm, qin, in_sem.at[0])
    cp_t = pltpu.make_async_copy(dt_hbm, dtin, in_sem.at[1])
    cp_q.start()
    cp_t.start()

    barrier = pltpu.get_barrier_semaphore()
    for d in range(1, nx):
        pl.semaphore_signal(barrier, inc=1, device_id=(lax.rem(ix + d, nx), iy), device_id_type=MESH)

    @pl.when(has_d)
    def _():
        pl.semaphore_signal(barrier, inc=1, device_id=(ix, iy - 1), device_id_type=MESH)

    @pl.when(has_u)
    def _():
        pl.semaphore_signal(barrier, inc=1, device_id=(ix, iy + 1), device_id_type=MESH)

    def remote(src, dst, s_sem, r_sem, target):
        return pltpu.make_async_remote_copy(
            src_ref=src, dst_ref=dst, send_sem=s_sem, recv_sem=r_sem,
            device_id=target, device_id_type=MESH,
        )

    right_x = (lax.rem(ix + 1, nx), iy)
    left_x = (lax.rem(ix + nx - 1, nx), iy)
    up_y = (ix, lax.rem(iy + 1, ny))
    down_y = (ix, lax.rem(iy + ny - 1, ny))
    hx_to_r = remote(q_hbm.at[:, pl.ds(rows - 8, 8), :], hl, hx_send.at[0], hx_recv.at[0], right_x)
    hx_to_l = remote(q_hbm.at[:, pl.ds(0, 8), :], hr, hx_send.at[1], hx_recv.at[1], left_x)
    w_to_u = remote(wsend, wl, wy_send.at[0], wy_recv.at[0], up_y)
    w_to_d = remote(wsend, wr, wy_send.at[1], wy_recv.at[1], down_y)

    if ny > 1:
        both = jnp.logical_and(has_d, has_u)

        @pl.when(both)
        def _():
            pl.semaphore_wait(barrier, nx + 1)

        @pl.when(jnp.logical_not(both))
        def _():
            pl.semaphore_wait(barrier, nx)
    else:
        pl.semaphore_wait(barrier, nx - 1)

    pl.when(has_r)(hx_to_r.start)
    pl.when(has_l)(hx_to_l.start)

    @pl.when(jnp.logical_not(has_l))
    def _():
        hl[...] = jnp.zeros_like(hl)

    @pl.when(jnp.logical_not(has_r))
    def _():
        hr[...] = jnp.zeros_like(hr)

    @pl.when(jnp.logical_not(has_d))
    def _():
        wl[...] = jnp.zeros_like(wl)

    @pl.when(jnp.logical_not(has_u))
    def _():
        wr[...] = jnp.zeros_like(wr)

    if nx < 8:
        gath[pl.ds(nx * ROWS_PACK, (8 - nx) * ROWS_PACK), :] = jnp.zeros(
            ((8 - nx) * ROWS_PACK, 128), jnp.float32
        )

    shape = (8, 128)
    lane = lax.broadcasted_iota(jnp.int32, shape, 1)
    sub = lax.broadcasted_iota(jnp.int32, shape, 0)
    zero = jnp.where(lane + sub < 0, 1.0, 0.0)
    one = jnp.where(lane + sub < 0, 0.0, 1.0)
    cp_q.wait()
    cp_t.wait()

    def store_x(t, q, u, p):
        fx = flux_x(q, u, p)
        for k in range(5):
            eqs[k, t] = EPS * q[k]
            fs[k, t] = (1.0 / 12.0) * fx[k]

    for base in range(0, T, 32):
        def first(t, packs):
            q = [qin[k, pl.ds(t, 8, stride=T), :] for k in range(5)]
            u, v, w, p, c2 = primitive(q)
            rc = lax.rsqrt(c2)
            us[t + 2] = u
            vs[t] = v
            ws[t] = w
            cs[t + 2] = c2 * rc
            rcs[t] = rc
            store_x(t + 2, q, u, p)
            fy = flux_y(q, v, p)
            shift = 2 + 4 * (t - base)
            fresh = []
            for k in range(5):
                f = (1.0 / 12.0) * fy[k]
                e = EPS * q[k]
                f2 = f + f
                r_m2 = pltpu.roll(f + e, 2, 1)
                r_m1 = pltpu.roll(-4.0 * (f2 + e), 1, 1)
                r_p1 = pltpu.roll(4.0 * (f2 - e), 127, 1)
                r_p2 = pltpu.roll(e - f, 126, 1)
                wrap = jnp.where(lane < 1, r_m1, jnp.where(lane > 126, r_p1, 0.0)) + jnp.where(
                    lane < 2, r_m2, jnp.where(lane > 125, r_p2, 0.0)
                )
                total = (r_m2 + r_p2) + (r_m1 + r_p1) + 6.0 * e
                res[k, t] = total - wrap
                fresh.append(packs[k] + pltpu.roll(wrap, shift, 1))
            return tuple(fresh)

        packs = lax.fori_loop(base, min(base + 32, T), first, (zero,) * 5)
        for k in range(5):
            wsend[base // 32, k] = packs[k]

    pl.when(has_u)(w_to_u.start)
    pl.when(has_d)(w_to_d.start)

    pl.when(has_l)(hx_to_r.wait_recv)
    pl.when(has_r)(hx_to_l.wait_recv)

    for t in (-2, -1, T, T + 1):
        q = []
        for k in range(5):
            if t < 0:
                edge = hl[k] if t == -1 else pltpu.roll(hl[k], 1, 0)
                mine = qin[k, pl.ds(T + t, 8, stride=T), :]
                q.append(pltpu.roll(jnp.where(sub == 7, edge, mine), 1, 0))
            else:
                edge = hr[k] if t == T else pltpu.roll(hr[k], 7, 0)
                mine = qin[k, pl.ds(t - T, 8, stride=T), :]
                q.append(pltpu.roll(jnp.where(sub == 0, edge, mine), 7, 0))
        if t < 0:
            outside = jnp.logical_and(sub == 0, ix == 0)
        else:
            outside = jnp.logical_and(sub == 7, ix == nx - 1)
        u, v, w, p, c2 = primitive([jnp.where(outside, 1.0, q[0])] + q[1:])
        us[t + 2] = u
        cs[t + 2] = jnp.sqrt(jnp.where(outside, 1.0, c2))
        store_x(t + 2, q, u, p)

    def matrix_step(t, carry):
        for k in range(5):
            f = [fs[k, t + j] for j in (0, 1, 3, 4)]
            e = [eqs[k, t + j] for j in range(5)]
            x = (
                (f[0] - f[3]) + (e[0] + e[4])
                + (8.0 * (f[2] - f[1]) - 4.0 * (e[1] + e[3])) + 6.0 * e[2]
            )
            res[k, t] = res[k, t] + x
        dt = dtin[pl.ds(t, 8, stride=T), :]
        diag = 8.0 / dt + 6.0
        su = [us[t + 1 + j] for j in range(3)]
        sc = [cs[t + 1 + j] for j in range(3)]
        lu, uu = su[0] + su[1], su[1] + su[2]
        lc, uc = sc[0] + sc[1], sc[1] + sc[2]
        fresh = []
        for m in range(3):
            p1, p2, q1, q2, a1, a2, b1, b2, al0, be0, ah0, bh0, al1, be1, ah1, bh1 = carry[m]
            if m == 0:
                lo, up = lu, uu
            elif m == 1:
                lo, up = lu + lc, uu + uc
            else:
                lo, up = lu - lc, uu - uc
            low = -2.0 * lo - 4.0
            upp = 2.0 * up - 4.0
            rl = low - p2
            piv = (diag - q2) - rl * p1
            inv = 1.0 / piv
            p0 = (upp - rl * q1) * inv
            a0 = -(a2 + rl * a1) * inv
            b0 = -(b2 + rl * b1) * inv
            mat[7 * m + 0, t] = p0
            mat[7 * m + 1, t] = inv
            mat[7 * m + 2, t] = a0
            mat[7 * m + 3, t] = b0
            mat[7 * m + 4, t] = rl
            mat[7 * m + 5, t] = al0
            mat[7 * m + 6, t] = al1
            fresh.append(
                (
                    p0, p1, inv, q1, a0, a1, b0, b1,
                    be0 - al0 * p0, -al0 * inv, ah0 - al0 * a0, bh0 - al0 * b0,
                    be1 - al1 * p0, -al1 * inv, ah1 - al1 * a0, bh1 - al1 * b0,
                )
            )
        return tuple(fresh)

    start = (
        zero, zero, zero, zero, zero, -one, -one, zero,
        -one, zero, zero, zero, zero, -one, zero, zero,
    )
    ends = lax.fori_loop(0, T, matrix_step, (start,) * 3)

    pl.when(has_d)(w_to_u.wait_recv)
    pl.when(has_u)(w_to_d.wait_recv)

    halo_lanes = jnp.logical_or(lane < 2, lane > 125)
    from_up = (lane & 3) < 2
    rhs_carry = ((zero, zero, zero, zero),) * 5
    for base in range(0, T, 32):
        inflow = [jnp.where(from_up, wr[base // 32, k], wl[base // 32, k]) for k in range(5)]

        def rhs_step(t, carry):
            shift = 126 - 4 * (t - base)
            r = []
            for k in range(5):
                got = jnp.where(halo_lanes, pltpu.roll(inflow[k], shift, 1), 0.0)
                r.append(-8.0 * (res[k, t] + got))
            u, v, w, rc = us[t + 2], vs[t], ws[t], rcs[t]
            s = u * u + v * v + w * w
            m = u * r[1] + v * r[2] + w * r[3]
            k2 = (0.4 * rc * rc) * ((0.5 * s) * r[0] - m + r[4])
            kk = 0.5 * k2
            a = (r[1] - u * r[0]) * (0.5 * rc)
            waves = [r[0] - k2, r[2] - v * r[0], r[3] - w * r[0], kk + a, kk - a]
            coef = [[mat[7 * mm_ + j, t] for j in (1, 4, 5, 6)] for mm_ in range(3)]
            fresh = []
            for f in range(5):
                inv, rl, al0, al1 = coef[FAMILY[f]]
                g1, g2, h0, h1 = carry[f]
                g0 = ((waves[f] - g2) - rl * g1) * inv
                gs[f, t] = g0
                fresh.append((g0, g1, h0 - al0 * g0, h1 - al1 * g0))
            return tuple(fresh)

        rhs_carry = lax.fori_loop(base, min(base + 32, T), rhs_step, rhs_carry)

    mats, rhs = [], []
    pieces = []
    for m in range(3):
        p1, p2, q1, q2, a1, a2, b1, b2, al0, be0, ah0, bh0, al1, be1, ah1, bh1 = ends[m]
        pieces.append(p2)
        mats.append(
            (
                (-ah0, -bh0, -ah1, -bh1),
                (-al0, -be0, -al1, -be1),
                (p2 * a1 - a2, p2 * b1 - b2, -a1, -b1),
                (p2 * p1 - q2, p2 * q1, -p1, -q1),
            )
        )
    for f in range(5):
        g1, g2, h0, h1 = rhs_carry[f]
        rhs.append(((h0, h1), (g2 - pieces[FAMILY[f]] * g1, g1)))

    inner = (1, 2, 4)
    mats, rhs, records = reduce_levels(mats, rhs, inner, False)
    flat, tree = jax.tree.flatten((mats, rhs))
    for i, x in enumerate(flat):
        pack[i : i + 1, :] = x[0:1, :]
    mine = pl.ds(pl.multiple_of(ix * ROWS_PACK, 8), ROWS_PACK)
    gathers = [
        remote(pack, gath.at[mine, :], g_send.at[d - 1], g_recv.at[d - 1], (lax.rem(ix + d, nx), iy))
        for d in range(1, nx)
    ]
    for g in gathers:
        g.start()
    own = pltpu.make_async_copy(pack, gath.at[mine, :], in_sem.at[2])
    own.start()
    own.wait()
    for g in gathers:
        g.wait_recv()
    top = [gath[pl.ds(i, 8, stride=ROWS_PACK), :] for i in range(len(flat))]
    t_mats, t_rhs = jax.tree.unflatten(tree, top)
    outer = []
    d = 1
    while d < nx:
        outer.append(d)
        d *= 2
    _, _, t_records = reduce_levels(t_mats, t_rhs, outer, True)
    left, right = expand_levels(t_records, outer, [None] * 5, [None] * 5, sub, True)
    turn = lax.rem(8 - ix, 8)
    left = [tuple(pltpu.roll(x, turn, 0) for x in pair) for pair in left]
    right = [tuple(pltpu.roll(x, turn, 0) for x in pair) for pair in right]
    left, right = expand_levels(records, inner, left, right, sub, False)

    def back_step(i, carry):
        t = T - 1 - i
        coef = [[mat[7 * m + j, t] for j in range(4)] for m in range(3)]
        fresh, x = [], []
        for f in range(5):
            p0, q0, a0, b0 = coef[FAMILY[f]]
            x1, x2 = carry[f]
            l2, l1 = left[f]
            x0 = (gs[f, t] - a0 * l2 - b0 * l1) - p0 * x1 - q0 * x2
            x.append(x0)
            fresh.append((x0, x1))
        u, v, w, c = us[t + 2], vs[t], ws[t], cs[t + 2]
        hs = 0.5 * (u * u + v * v + w * w)
        tt = x[3] + x[4]
        dd = c * (x[3] - x[4])
        base_sum = x[0] + tt
        oo = [
            base_sum,
            u * base_sum + dd,
            v * base_sum + x[1],
            w * base_sum + x[2],
            hs * base_sum + v * x[1] + w * x[2] + 2.5 * (c * c) * tt + u * dd,
        ]
        for k in range(5):
            oout[k, pl.ds(t, 8, stride=T), :] = oo[k]
        return tuple(fresh)

    lax.fori_loop(0, T, back_step, tuple((right[f][0], right[f][1]) for f in range(5)))
    cp_o = pltpu.make_async_copy(oout, out_hbm, out_sem.at[0])
    cp_o.start()
    for g in gathers:
        g.wait_send()
    pl.when(has_r)(hx_to_r.wait_send)
    pl.when(has_l)(hx_to_l.wait_send)
    pl.when(has_u)(w_to_u.wait_send)
    pl.when(has_d)(w_to_d.wait_send)
    cp_o.wait()


def on_device(nx, ny, conserved, time_step):
    rows, cols = conserved.shape[2], conserved.shape[3]
    groups = rows // 8
    blocks = -(-groups // 32)
    f32 = jnp.float32
    vm = lambda *s: pltpu.VMEM(s + (8, 128), f32)
    out = pl.pallas_call(
        functools.partial(kernel, nx, ny, rows),
        out_shape=jax.ShapeDtypeStruct((5, rows, cols), f32),
        in_specs=[pl.BlockSpec(memory_space=pl.ANY)] * 2,
        out_specs=pl.BlockSpec(memory_space=pl.ANY),
        scratch_shapes=[
            pltpu.VMEM((5, rows, cols), f32),
            pltpu.VMEM((rows, cols), f32),
            pltpu.VMEM((5, rows, cols), f32),
            vm(5), vm(5),
            vm(5, groups + 4), vm(5, groups + 4), vm(groups + 4),
            vm(groups), vm(groups), vm(groups + 4), vm(groups),
            vm(5, groups), vm(21, groups), vm(5, groups),
            vm(blocks, 5), vm(blocks, 5), vm(blocks, 5),
            pltpu.VMEM((ROWS_PACK, 128), f32),
            pltpu.VMEM((8 * ROWS_PACK, 128), f32),
            pltpu.SemaphoreType.DMA((3,)),
            pltpu.SemaphoreType.DMA((1,)),
            pltpu.SemaphoreType.DMA((2,)),
            pltpu.SemaphoreType.DMA((2,)),
            pltpu.SemaphoreType.DMA((2,)),
            pltpu.SemaphoreType.DMA((2,)),
            pltpu.SemaphoreType.DMA((max(nx - 1, 1),)),
            pltpu.SemaphoreType.DMA((max(nx - 1, 1),)),
        ],
        compiler_params=pltpu.CompilerParams(
            collective_id=0, has_side_effects=True, vmem_limit_bytes=40 * 1024 * 1024
        ),
    )(conserved.reshape(5, rows, cols), time_step.reshape(rows, cols))
    return out.reshape(conserved.shape)


def solution(mesh):
    return jax.shard_map(
        functools.partial(on_device, mesh.shape["gx"], mesh.shape["gy"]),
        mesh=mesh,
        in_specs=(P(None, None, "gx", "gy"), P(None, "gx", "gy")),
        out_specs=P(None, None, "gx", "gy"),
        check_vma=False,
    )
```

profile of v0, /device:TPU:0, one launch (start us, length us, event | category | flops | bytes accessed | tf_op | source)
XLA Modules:
  0.0 28.4 jit_solution(16304432788730034252)
XLA Ops:
  0.0 0.0 copy-start
  0.0 1.2 %copy-done = f32[5,1,384,128]{3,2,1,0:T(8,128)S(1)} copy-done((f32[5,1,384,128]{3,2,1,0:T(8,128)S(1)}, f32[5,1,384,128]{3,2,1,0:T(8,128)}, u32[]{:S(2)}) %copy-start) | copy-done | bytes 983064
  1.2 0.0 copy-start.1
  1.2 0.9 %copy-done.1 = f32[1,384,128]{2,1,0:T(8,128)S(1)} copy-done((f32[1,384,128]{2,1,0:T(8,128)S(1)}, f32[1,384,128]{2,1,0:T(8,128)}, u32[]{:S(2)}) %copy-start.1) | copy-done | bytes 196632
  2.1 25.3 %shard_map.28 = f32[5,384,128]{2,1,0:T(8,128)S(1)} custom-call(f32[5,384,128]{2,1,0:T(8,128)S(1)} %bitcast.6, f32[384,128]{1,0:T(8,128)S(1)} %bitcast.7), custom_call_target="tpu_custom_call" | custom-call | tf_op jit(solution)/shard_map/pallas_call | solution.py:455
  27.5 0.9 %copy.5 = f32[5,1,384,128]{3,2,1,0:T(8,128)} copy(f32[5,1,384,128]{3,2,1,0:T(8,128)S(1)} %bitcast.5) | data formatting | bytes 1966080
Async XLA Ops:
  0.0 1.2 %copy-start = (f32[5,1,384,128]{3,2,1,0:T(8,128)S(1)}, f32[5,1,384,128]{3,2,1,0:T(8,128)}, u32[]{:S(2)}) copy-start(f32[5,1,384,128]{3,2,1,0:T(8,128)} %param.2) | copy-start | bytes 2949124
  1.2 0.9 %copy-start.1 = (f32[1,384,128]{2,1,0:T(8,128)S(1)}, f32[1,384,128]{2,1,0:T(8,128)}, u32[]{:S(2)}) copy-start(f32[1,384,128]{2,1,0:T(8,128)} %param.3) | copy-start | bytes 589828
where the time goes:
time: 28.6 us; the launch traced here: 28.4 us
  Pallas kernels  25.3 us (88%)
  local copies, waits for them, and re-layouts  3.07 us (11%)
    pallas_call x1, Pallas kernels, on_device(): pl.pallas_call(functools.partial(kernel, nx, ny, rows), out_shape=jax.Sha...  25.3 us
    unnamed x5, local copies, waits for them, and re-layouts  3.07 us

commit v1 on v0

--- a/solution.py
+++ b/solution.py
@@ -8,7 +8,8 @@
 
 EPS = 0.02
 MESH = pl.DeviceIdType.MESH
-ROWS_PACK = 72
+ROWS_M = 48
+ROWS_R = 24
 FAMILY = (0, 0, 0, 1, 2)
 
 
@@ -54,8 +55,8 @@
     return (m3 * r, -m1 * r, -m2 * r, m0 * r)
 
 
-def merge(mats_a, mats_b, rhs_a, rhs_b, last=False):
-    mats, rec_m, invs = [], [], []
+def merge_mats(mats_a, mats_b, last):
+    mats, rec, invs = [], [], []
     for (hl_a, hr_a, tl_a, tr_a), (hl_b, hr_b, tl_b, tr_b) in zip(mats_a, mats_b):
         minv = schur_inverse(tr_a, hl_b)
         invs.append(minv)
@@ -73,30 +74,41 @@
                 add(tr_b, mm(tl_b, tail_r)),
             )
         )
-        rec_m.append((head_l, head_r, tail_l, tail_r))
-    rhs, rec_y = [], []
+        rec.append((head_l, head_r, tail_l, tail_r))
+    return mats, (mats_a, mats_b, invs, rec)
+
+
+def merge_rhs(level, rhs_a, rhs_b, last):
+    mats_a, mats_b, invs, _ = level
+    rhs, rec = [], []
     for f, ((h_a, t_a), (h_b, t_b)) in enumerate(zip(rhs_a, rhs_b)):
         m = FAMILY[f]
-        hl_b, tr_a = mats_b[m][0], mats_a[m][3]
-        head_y = mv(invs[m], add(h_b, mv(hl_b, t_a)))
-        tail_y = add(t_a, mv(tr_a, head_y))
-        rec_y.append((head_y, tail_y))
+        head_y = mv(invs[m], add(h_b, mv(mats_b[m][0], t_a)))
+        tail_y = add(t_a, mv(mats_a[m][3], head_y))
+        rec.append((head_y, tail_y))
         if not last:
             rhs.append((add(h_a, mv(mats_a[m][1], head_y)), add(t_b, mv(mats_b[m][2], tail_y))))
-    return mats, rhs, (rec_m, rec_y)
+    return rhs, rec
 
 
 def shifted(tree, d):
     return jax.tree.map(lambda x: pltpu.roll(x, 8 - d, 0), tree)
 
 
-def reduce_levels(mats, rhs, strides, root):
+def reduce_mats(mats, strides, root):
+    levels = []
+    for d in strides:
+        mats, level = merge_mats(mats, shifted(mats, d), root and d == strides[-1])
+        levels.append(level)
+    return mats, levels
+
+
+def reduce_rhs(levels, rhs, strides, root):
     records = []
-    for d in strides:
-        last = root and d == strides[-1]
-        mats, rhs, rec = merge(mats, shifted(mats, d), rhs, shifted(rhs, d), last)
-        records.append(rec)
-    return mats, rhs, records
+    for level, d in zip(levels, strides):
+        rhs, rec = merge_rhs(level, rhs, shifted(rhs, d), root and d == strides[-1])
+        records.append((level[3], rec))
+    return rhs, records
 
 
 def expand_levels(records, strides, left, right, sub, root):
@@ -118,20 +130,16 @@
 
 def kernel(
     nx, ny, rows,
-    q_hbm, dt_hbm, out_hbm,
-    qin, dtin, oout, hl, hr, eqs, fs, us, vs, ws, cs, rcs, res, mat, gs,
-    wsend, wl, wr, pack, gath,
-    in_sem, out_sem, hx_send, hx_recv, wy_send, wy_recv, g_send, g_recv,
+    qin, dtin, oout,
+    hl, hr, eqs, fs, us, vs, ws, cs, rcs, res, mat, gs,
+    wsend, wl, wr, pack_m, gath_m, pack_r, gath_r,
+    in_sem, hx_send, hx_recv, wy_send, wy_recv, gm_send, gm_recv, gr_send, gr_recv,
 ):
     T = rows // 8
     ix = lax.axis_index("gx")
     iy = lax.axis_index("gy")
     has_l, has_r = ix > 0, ix < nx - 1
     has_d, has_u = iy > 0, iy < ny - 1
-    cp_q = pltpu.make_async_copy(q_hbm, qin, in_sem.at[0])
-    cp_t = pltpu.make_async_copy(dt_hbm, dtin, in_sem.at[1])
-    cp_q.start()
-    cp_t.start()
 
     barrier = pltpu.get_barrier_semaphore()
     for d in range(1, nx):
@@ -155,8 +163,8 @@
     left_x = (lax.rem(ix + nx - 1, nx), iy)
     up_y = (ix, lax.rem(iy + 1, ny))
     down_y = (ix, lax.rem(iy + ny - 1, ny))
-    hx_to_r = remote(q_hbm.at[:, pl.ds(rows - 8, 8), :], hl, hx_send.at[0], hx_recv.at[0], right_x)
-    hx_to_l = remote(q_hbm.at[:, pl.ds(0, 8), :], hr, hx_send.at[1], hx_recv.at[1], left_x)
+    hx_to_r = remote(qin.at[:, pl.ds(rows - 8, 8), :], hl, hx_send.at[0], hx_recv.at[0], right_x)
+    hx_to_l = remote(qin.at[:, pl.ds(0, 8), :], hr, hx_send.at[1], hx_recv.at[1], left_x)
     w_to_u = remote(wsend, wl, wy_send.at[0], wy_recv.at[0], up_y)
     w_to_d = remote(wsend, wr, wy_send.at[1], wy_recv.at[1], down_y)
 
@@ -193,17 +201,15 @@
         wr[...] = jnp.zeros_like(wr)
 
     if nx < 8:
-        gath[pl.ds(nx * ROWS_PACK, (8 - nx) * ROWS_PACK), :] = jnp.zeros(
-            ((8 - nx) * ROWS_PACK, 128), jnp.float32
-        )
-
+        for gath, n in ((gath_m, ROWS_M), (gath_r, ROWS_R)):
+            gath[pl.ds(nx * n, (8 - nx) * n), :] = jnp.zeros(((8 - nx) * n, 128), jnp.float32)
+
+    pack_r[16:24, :] = jnp.zeros((8, 128), jnp.float32)
     shape = (8, 128)
     lane = lax.broadcasted_iota(jnp.int32, shape, 1)
     sub = lax.broadcasted_iota(jnp.int32, shape, 0)
     zero = jnp.where(lane + sub < 0, 1.0, 0.0)
     one = jnp.where(lane + sub < 0, 0.0, 1.0)
-    cp_q.wait()
-    cp_t.wait()
 
     def store_x(t, q, u, p):
         fx = flux_x(q, u, p)
@@ -241,7 +247,7 @@
                 fresh.append(packs[k] + pltpu.roll(wrap, shift, 1))
             return tuple(fresh)
 
-        packs = lax.fori_loop(base, min(base + 32, T), first, (zero,) * 5)
+        packs = lax.fori_loop(base, min(base + 32, T), first, (zero,) * 5, unroll=4)
         for k in range(5):
             wsend[base // 32, k] = packs[k]
 
@@ -323,7 +329,53 @@
         zero, zero, zero, zero, zero, -one, -one, zero,
         -one, zero, zero, zero, zero, -one, zero, zero,
     )
-    ends = lax.fori_loop(0, T, matrix_step, (start,) * 3)
+    ends = lax.fori_loop(0, T, matrix_step, (start,) * 3, unroll=4)
+
+    mats = []
+    pieces = []
+    for m in range(3):
+        p1, p2, q1, q2, a1, a2, b1, b2, al0, be0, ah0, bh0, al1, be1, ah1, bh1 = ends[m]
+        pieces.append(p2)
+        mats.append(
+            (
+                (-ah0, -bh0, -ah1, -bh1),
+                (-al0, -be0, -al1, -be1),
+                (p2 * a1 - a2, p2 * b1 - b2, -a1, -b1),
+                (p2 * p1 - q2, p2 * q1, -p1, -q1),
+            )
+        )
+    inner = (1, 2, 4)
+    outer = []
+    d = 1
+    while d < nx:
+        outer.append(d)
+        d *= 2
+    mats, levels = reduce_mats(mats, inner, False)
+
+    def exchange(tree, pack, gath, n_rows, g_send, g_recv, own_sem):
+        flat, form = jax.tree.flatten(tree)
+        for i, x in enumerate(flat):
+            pack[i : i + 1, :] = x[0:1, :]
+        mine = gath.at[pl.ds(pl.multiple_of(ix * n_rows, 8), n_rows), :]
+        copies = [
+            remote(pack, mine, g_send.at[d - 1], g_recv.at[d - 1], (lax.rem(ix + d, nx), iy))
+            for d in range(1, nx)
+        ]
+        for g in copies:
+            g.start()
+        own = pltpu.make_async_copy(pack, mine, own_sem)
+        own.start()
+
+        def finish():
+            own.wait()
+            for g in copies:
+                g.wait_recv()
+            top = [gath[pl.ds(i, 8, stride=n_rows), :] for i in range(len(flat))]
+            return jax.tree.unflatten(form, top)
+
+        return copies, finish
+
+    copies_m, finish_m = exchange(mats, pack_m, gath_m, ROWS_M, gm_send, gm_recv, in_sem.at[0])
 
     pl.when(has_d)(w_to_u.wait_recv)
     pl.when(has_u)(w_to_d.wait_recv)
@@ -357,50 +409,17 @@
                 fresh.append((g0, g1, h0 - al0 * g0, h1 - al1 * g0))
             return tuple(fresh)
 
-        rhs_carry = lax.fori_loop(base, min(base + 32, T), rhs_step, rhs_carry)
-
-    mats, rhs = [], []
-    pieces = []
-    for m in range(3):
-        p1, p2, q1, q2, a1, a2, b1, b2, al0, be0, ah0, bh0, al1, be1, ah1, bh1 = ends[m]
-        pieces.append(p2)
-        mats.append(
-            (
-                (-ah0, -bh0, -ah1, -bh1),
-                (-al0, -be0, -al1, -be1),
-                (p2 * a1 - a2, p2 * b1 - b2, -a1, -b1),
-                (p2 * p1 - q2, p2 * q1, -p1, -q1),
-            )
-        )
+        rhs_carry = lax.fori_loop(base, min(base + 32, T), rhs_step, rhs_carry, unroll=8)
+
+    rhs = []
     for f in range(5):
         g1, g2, h0, h1 = rhs_carry[f]
         rhs.append(((h0, h1), (g2 - pieces[FAMILY[f]] * g1, g1)))
 
-    inner = (1, 2, 4)
-    mats, rhs, records = reduce_levels(mats, rhs, inner, False)
-    flat, tree = jax.tree.flatten((mats, rhs))
-    for i, x in enumerate(flat):
-        pack[i : i + 1, :] = x[0:1, :]
-    mine = pl.ds(pl.multiple_of(ix * ROWS_PACK, 8), ROWS_PACK)
-    gathers = [
-        remote(pack, gath.at[mine, :], g_send.at[d - 1], g_recv.at[d - 1], (lax.rem(ix + d, nx), iy))
-        for d in range(1, nx)
-    ]
-    for g in gathers:
-        g.start()
-    own = pltpu.make_async_copy(pack, gath.at[mine, :], in_sem.at[2])
-    own.start()
-    own.wait()
-    for g in gathers:
-        g.wait_recv()
-    top = [gath[pl.ds(i, 8, stride=ROWS_PACK), :] for i in range(len(flat))]
-    t_mats, t_rhs = jax.tree.unflatten(tree, top)
-    outer = []
-    d = 1
-    while d < nx:
-        outer.append(d)
-        d *= 2
-    _, _, t_records = reduce_levels(t_mats, t_rhs, outer, True)
+    rhs, records = reduce_rhs(levels, rhs, inner, False)
+    copies_r, finish_r = exchange(rhs, pack_r, gath_r, ROWS_R, gr_send, gr_recv, in_sem.at[1])
+    _, t_levels = reduce_mats(finish_m(), outer, True)
+    _, t_records = reduce_rhs(t_levels, finish_r(), outer, True)
     left, right = expand_levels(t_records, outer, [None] * 5, [None] * 5, sub, True)
     turn = lax.rem(8 - ix, 8)
     left = [tuple(pltpu.roll(x, turn, 0) for x in pair) for pair in left]
@@ -434,16 +453,13 @@
             oout[k, pl.ds(t, 8, stride=T), :] = oo[k]
         return tuple(fresh)
 
-    lax.fori_loop(0, T, back_step, tuple((right[f][0], right[f][1]) for f in range(5)))
-    cp_o = pltpu.make_async_copy(oout, out_hbm, out_sem.at[0])
-    cp_o.start()
-    for g in gathers:
+    lax.fori_loop(0, T, back_step, tuple((right[f][0], right[f][1]) for f in range(5)), unroll=4)
+    for g in copies_m + copies_r:
         g.wait_send()
     pl.when(has_r)(hx_to_r.wait_send)
     pl.when(has_l)(hx_to_l.wait_send)
     pl.when(has_u)(w_to_u.wait_send)
     pl.when(has_d)(w_to_d.wait_send)
-    cp_o.wait()
 
 
 def on_device(nx, ny, conserved, time_step):
@@ -455,25 +471,25 @@
     out = pl.pallas_call(
         functools.partial(kernel, nx, ny, rows),
         out_shape=jax.ShapeDtypeStruct((5, rows, cols), f32),
-        in_specs=[pl.BlockSpec(memory_space=pl.ANY)] * 2,
-        out_specs=pl.BlockSpec(memory_space=pl.ANY),
+        in_specs=[pl.BlockSpec(memory_space=pltpu.VMEM)] * 2,
+        out_specs=pl.BlockSpec(memory_space=pltpu.VMEM),
         scratch_shapes=[
-            pltpu.VMEM((5, rows, cols), f32),
-            pltpu.VMEM((rows, cols), f32),
-            pltpu.VMEM((5, rows, cols), f32),
             vm(5), vm(5),
             vm(5, groups + 4), vm(5, groups + 4), vm(groups + 4),
             vm(groups), vm(groups), vm(groups + 4), vm(groups),
             vm(5, groups), vm(21, groups), vm(5, groups),
             vm(blocks, 5), vm(blocks, 5), vm(blocks, 5),
-            pltpu.VMEM((ROWS_PACK, 128), f32),
-            pltpu.VMEM((8 * ROWS_PACK, 128), f32),
-            pltpu.SemaphoreType.DMA((3,)),
-            pltpu.SemaphoreType.DMA((1,)),
+            pltpu.VMEM((ROWS_M, 128), f32),
+            pltpu.VMEM((8 * ROWS_M, 128), f32),
+            pltpu.VMEM((ROWS_R, 128), f32),
+            pltpu.VMEM((8 * ROWS_R, 128), f32),
             pltpu.SemaphoreType.DMA((2,)),
             pltpu.SemaphoreType.DMA((2,)),
             pltpu.SemaphoreType.DMA((2,)),
             pltpu.SemaphoreType.DMA((2,)),
+            pltpu.SemaphoreType.DMA((2,)),
+            pltpu.SemaphoreType.DMA((max(nx - 1, 1),)),
+            pltpu.SemaphoreType.DMA((max(nx - 1, 1),)),
             pltpu.SemaphoreType.DMA((max(nx - 1, 1),)),
             pltpu.SemaphoreType.DMA((max(nx - 1, 1),)),
         ],

time: 28.6 us -> 18.2 us (0.64)
  Pallas kernels: 25.3 us -> 14.9 us
    pallas_call x1, Pallas kernels: 25.3 us -> 14.9 us  [on_device(): pl.pallas_call(functools.partial(kernel, nx, ny, rows), out_shape=jax.Sha...]
where the time goes in v1:
time: 18.2 us; the launch traced here: 18 us
  Pallas kernels  14.9 us (82%)
  local copies, waits for them, and re-layouts  3.07 us (17%)
    pallas_call x1, Pallas kernels, on_device(): pl.pallas_call(functools.partial(kernel, nx, ny, rows), out_shape=jax.Sha...  14.9 us
    unnamed x5, local copies, waits for them, and re-layouts  3.07 us

profile of v1, /device:TPU:0, one launch (start us, length us, event | category | flops | bytes accessed | tf_op | source)
XLA Modules:
  0.0 18.0 jit_solution(3329508864833953919)
XLA Ops:
  0.0 0.0 copy-start
  0.0 1.2 %copy-done = f32[5,1,384,128]{3,2,1,0:T(8,128)S(1)} copy-done((f32[5,1,384,128]{3,2,1,0:T(8,128)S(1)}, f32[5,1,384,128]{3,2,1,0:T(8,128)}, u32[]{:S(2)}) %copy-start) | copy-done | bytes 983064
  1.2 0.0 copy-start.1
  1.2 0.9 %copy-done.1 = f32[1,384,128]{2,1,0:T(8,128)S(1)} copy-done((f32[1,384,128]{2,1,0:T(8,128)S(1)}, f32[1,384,128]{2,1,0:T(8,128)}, u32[]{:S(2)}) %copy-start.1) | copy-done | bytes 196632
  2.1 14.9 %shard_map.28 = f32[5,384,128]{2,1,0:T(8,128)S(1)} custom-call(f32[5,384,128]{2,1,0:T(8,128)S(1)} %bitcast.6, f32[384,128]{1,0:T(8,128)S(1)} %bitcast.7), custom_call_target="tpu_custom_call" | custom-call | tf_op jit(solution)/shard_map/pallas_call | solution.py:471
  17.1 0.9 %copy.5 = f32[5,1,384,128]{3,2,1,0:T(8,128)} copy(f32[5,1,384,128]{3,2,1,0:T(8,128)S(1)} %bitcast.5) | data formatting | bytes 1966080
Async XLA Ops:
  0.0 1.2 %copy-start = (f32[5,1,384,128]{3,2,1,0:T(8,128)S(1)}, f32[5,1,384,128]{3,2,1,0:T(8,128)}, u32[]{:S(2)}) copy-start(f32[5,1,384,128]{3,2,1,0:T(8,128)} %param.2) | copy-start | bytes 2949124
  1.2 0.9 %copy-start.1 = (f32[1,384,128]{2,1,0:T(8,128)S(1)}, f32[1,384,128]{2,1,0:T(8,128)}, u32[]{:S(2)}) copy-start(f32[1,384,128]{2,1,0:T(8,128)} %param.3) | copy-start | bytes 589828
